TPU v7x, 32 devices: a whole 2x2x4 slice. The times are simulated.
32 devices in a mesh: rep: 2 (over x), node: 8 (over z, y), local: 2 (over core).
Axes of the slice: x: 2, y: 2, z: 4, core: 2. Of those that a mesh axis runs over, the one named last changes fastest.
Arguments:
- tokens: bfloat16 [4096, 1024], P(('rep', 'node', 'local')), parts along dimension 0, may hold values from -6 to 6
- grad_out: bfloat16 [4096, 1024], P(('rep', 'node', 'local')), parts along dimension 0, may hold values from -0.59765625 to 0.59765625
- expert_ids: int32 [4096, 8], P(('rep', 'node', 'local')), parts along dimension 0, may hold values from 0 to 31, as said below
- gate_values: bfloat16 [4096, 8], P(('rep', 'node', 'local')), parts along dimension 0, may hold values from 0.049804688 to 1
- w_gate: bfloat16 [32, 1024, 384], P('node', None, 'local'), may hold values from -0.1875 to 0.1875
- w_up: bfloat16 [32, 1024, 384], P('node', None, 'local'), may hold values from -0.1875 to 0.1875
- w_down: bfloat16 [32, 384, 1024], P('node', 'local'), may hold values from -0.3125 to 0.3125
Outputs:
- grad_tokens: bfloat16 [4096, 1024], P(('rep', 'node', 'local')), parts along dimension 0
- grad_gates: float32 [4096, 8], P(('rep', 'node', 'local')), parts along dimension 0
- grad_w_gate: bfloat16 [64, 1024, 384], P(('rep', 'node'), None, 'local'), parts along dimension 0
- grad_w_up: bfloat16 [64, 1024, 384], P(('rep', 'node'), None, 'local'), parts along dimension 0
- grad_w_down: bfloat16 [64, 384, 1024], P(('rep', 'node'), 'local'), parts along dimension 0
There are 2 independent parts, one for each index of `rep`. A program takes and returns all parts, laid end to end along the dimension named above; an argument that names none is the same for every part. Nothing has to cross between parts.
Inputs may be any that keep to these rules, and one draw needn't show every extreme that they name: `expert_ids`: expert e belongs to group e // 4. Each token names 8 different experts lying in exactly 4 different groups, one to three of each. Among the tokens of one device at most 96 reach any one group and at most 192 of their pairs name that group's experts; in the tokens of every device some group is reached by exactly 96 tokens with exactly 192 pairs.
All inputs are finite; a program needn't handle non-finite values.
Results may differ from a plain program's by a relative error of at most 0.0058.
Values may be sent and summed in bfloat16 or wider, within the bound.
A program may use at most 128 MiB of HBM per device.

v0:
```python
import jax
import jax.numpy as jnp
from jax import lax
from jax.sharding import PartitionSpec as P

LIMIT = 4


def silu_terms(pre_gate):
    sigma = jax.nn.sigmoid(pre_gate)
    return (pre_gate * sigma, sigma * (1.0 + pre_gate * (1.0 - sigma)))


def block_rows(rows_in, rows_grad, gate_column, gate_weight, up_weight, down_weight):
    pre_gate = jnp.dot(rows_in, gate_weight, preferred_element_type=jnp.float32)
    pre_up = jnp.dot(rows_in, up_weight, preferred_element_type=jnp.float32)
    activated, slope = silu_terms(pre_gate)
    hidden = (activated * pre_up).astype(jnp.bfloat16)
    back_hidden = jnp.dot(rows_grad, down_weight.T, preferred_element_type=jnp.float32)
    gate_grad = jnp.sum(back_hidden * hidden.astype(jnp.float32), axis=1)
    scaled = gate_column[:, None] * back_hidden
    grad_pre_gate = (scaled * pre_up * slope).astype(jnp.bfloat16)
    grad_pre_up = (scaled * activated).astype(jnp.bfloat16)
    input_grad = jnp.dot(grad_pre_gate, gate_weight.T, preferred_element_type=jnp.float32)
    input_grad = input_grad + jnp.dot(grad_pre_up, up_weight.T, preferred_element_type=jnp.float32)
    return (input_grad, gate_grad, hidden, grad_pre_gate, grad_pre_up)


def process(rows_in, rows_grad, rows_gate, gate_weights, up_weights, down_weights, pair_bound):
    total_rows, model_width = rows_in.shape
    group_size = rows_gate.shape[1]
    unit_count = gate_weights.shape[2]
    block_limit = (pair_bound + 127 * group_size) // 128
    slot_count = block_limit * 128
    window = min(slot_count, (total_rows + 127) // 128 * 128)
    buffer_rows = slot_count + window
    live = (rows_gate != 0).astype(jnp.int32)
    counts = jnp.sum(live, axis=0)
    padded = (counts + 127) // 128 * 128
    pad_start = jnp.cumsum(padded) - padded
    rank = jnp.cumsum(live, axis=0) - 1
    target = jnp.where(live == 1, pad_start[None, :] + rank, buffer_rows).reshape(-1)
    row_ids = jnp.broadcast_to(
        jnp.arange(total_rows, dtype=jnp.int32)[:, None], live.shape
    ).reshape(-1)
    slot_row = jnp.zeros(buffer_rows, jnp.int32).at[target].set(row_ids, mode="drop")
    slot_gate = (
        jnp.zeros(buffer_rows, jnp.float32)
        .at[target]
        .set(rows_gate.astype(jnp.float32).reshape(-1), mode="drop")
    )
    slot_live = jnp.zeros(buffer_rows, jnp.float32).at[target].set(1.0, mode="drop")
    block_first = jnp.arange(block_limit, dtype=jnp.int32) * 128
    block_expert = (
        jnp.sum((pad_start[None, :] <= block_first[:, None]).astype(jnp.int32), axis=1) - 1
    )
    slot_owner = jnp.concatenate(
        [jnp.repeat(block_expert, 128), jnp.full((window,), -1, jnp.int32)]
    )
    initial = (
        jnp.zeros((total_rows, model_width), jnp.float32),
        jnp.zeros((total_rows, group_size), jnp.float32),
        jnp.zeros((buffer_rows, unit_count), jnp.bfloat16),
        jnp.zeros((buffer_rows, unit_count), jnp.bfloat16),
        jnp.zeros((buffer_rows, unit_count), jnp.bfloat16),
    )

    def advance(index, state):
        input_state, gate_state, hidden_buf, gate_buf, up_buf = state
        first = index * 128
        rows = lax.dynamic_slice_in_dim(slot_row, first, 128, 0)
        gates = lax.dynamic_slice_in_dim(slot_gate, first, 128, 0)
        present = lax.dynamic_slice_in_dim(slot_live, first, 128, 0)
        expert = block_expert[index]
        results = block_rows(
            rows_in[rows],
            rows_grad[rows],
            gates,
            gate_weights[expert],
            up_weights[expert],
            down_weights[expert],
        )
        input_state = input_state.at[rows].add(results[0])
        gate_state = gate_state.at[rows, expert].add(present * results[1])
        hidden_buf = lax.dynamic_update_slice_in_dim(hidden_buf, results[2], first, 0)
        gate_buf = lax.dynamic_update_slice_in_dim(gate_buf, results[3], first, 0)
        up_buf = lax.dynamic_update_slice_in_dim(up_buf, results[4], first, 0)
        return (input_state, gate_state, hidden_buf, gate_buf, up_buf)

    final = lax.fori_loop(0, block_limit, advance, initial)
    hidden_buf, gate_buf, up_buf = (final[2], final[3], final[4])
    gate_list, up_list, down_list = ([], [], [])
    for expert in range(group_size):
        start = pad_start[expert]
        rows = lax.dynamic_slice_in_dim(slot_row, start, window, 0)
        mine = lax.dynamic_slice_in_dim(slot_owner, start, window, 0) == expert
        scale = jnp.where(mine, lax.dynamic_slice_in_dim(slot_gate, start, window, 0), 0.0)
        zero_unit = jnp.zeros((), jnp.bfloat16)
        grad_gate_rows = jnp.where(
            mine[:, None], lax.dynamic_slice_in_dim(gate_buf, start, window, 0), zero_unit
        )
        grad_up_rows = jnp.where(
            mine[:, None], lax.dynamic_slice_in_dim(up_buf, start, window, 0), zero_unit
        )
        hidden_rows = lax.dynamic_slice_in_dim(hidden_buf, start, window, 0)
        inputs = rows_in[rows]
        weighted_grad = (scale[:, None] * rows_grad[rows].astype(jnp.float32)).astype(jnp.bfloat16)
        gate_list.append(jnp.dot(inputs.T, grad_gate_rows, preferred_element_type=jnp.float32))
        up_list.append(jnp.dot(inputs.T, grad_up_rows, preferred_element_type=jnp.float32))
        down_list.append(jnp.dot(hidden_rows.T, weighted_grad, preferred_element_type=jnp.float32))
    return (final[0], final[1], (jnp.stack(gate_list), jnp.stack(up_list), jnp.stack(down_list)))


def on_device(tokens, grad_out, expert_ids, gate_values, w_gate, w_up, w_down):
    token_count, model_width = tokens.shape
    group_size = w_gate.shape[0]
    routed = expert_ids.shape[1]
    node_count = lax.axis_size("node")
    capacity = min(token_count, 3 * LIMIT * token_count // (2 * node_count))
    expert_count = group_size * node_count
    slot_total = node_count * capacity
    pair_bound = node_count * 2 * capacity
    hits = expert_ids[:, :, None] == jnp.arange(expert_count, dtype=jnp.int32)[None, None, :]
    gate_table = jnp.sum(jnp.where(hits, gate_values.astype(jnp.float32)[:, :, None], 0.0), axis=1)
    gate_table = gate_table.reshape(token_count, node_count, group_size)
    reached = jnp.any(
        jnp.any(hits, axis=1).reshape(token_count, node_count, group_size), axis=2
    ).astype(jnp.int32)
    position = jnp.cumsum(reached, axis=0) - 1
    matches = (reached[:, :, None] == 1) & (
        position[:, :, None] == jnp.arange(capacity, dtype=jnp.int32)[None, None, :]
    )
    sources = jnp.sum(
        jnp.where(matches, jnp.arange(token_count, dtype=jnp.int32)[:, None, None], 0), axis=0
    )
    filled = jnp.any(matches, axis=0)
    send_in = tokens[sources]
    send_grad = grad_out[sources]
    picked = gate_table[sources, jnp.arange(node_count, dtype=jnp.int32)[:, None]]
    send_gate = jnp.where(filled[:, :, None], picked, 0.0).astype(jnp.bfloat16)
    recv_in, recv_grad, recv_gate = (
        lax.all_to_all(send_in, "node", split_axis=0, concat_axis=0, tiled=True),
        lax.all_to_all(send_grad, "node", split_axis=0, concat_axis=0, tiled=True),
        lax.all_to_all(send_gate, "node", split_axis=0, concat_axis=0, tiled=True),
    )
    flat_in = recv_in.reshape(slot_total, model_width)
    flat_grad = recv_grad.reshape(slot_total, model_width)
    flat_gate = recv_gate.reshape(slot_total, group_size)
    whole_gate, whole_up, whole_down = (
        lax.all_gather(w_gate, "local", axis=2, tiled=True),
        lax.all_gather(w_up, "local", axis=2, tiled=True),
        lax.all_gather(w_down, "local", axis=1, tiled=True),
    )
    input_grad, gate_grad, weight_grads = process(
        flat_in, flat_grad, flat_gate, whole_gate, whole_up, whole_down, pair_bound
    )
    grad_w_gate, grad_w_up, grad_w_down = (
        lax.psum_scatter(weight_grads[0], "local", scatter_dimension=2, tiled=True),
        lax.psum_scatter(weight_grads[1], "local", scatter_dimension=2, tiled=True),
        lax.psum_scatter(weight_grads[2], "local", scatter_dimension=1, tiled=True),
    )
    back_in, back_gate = (
        lax.all_to_all(
            input_grad.reshape(node_count, capacity, model_width),
            "node",
            split_axis=0,
            concat_axis=0,
            tiled=True,
        ),
        lax.all_to_all(
            gate_grad.reshape(node_count, capacity, group_size),
            "node",
            split_axis=0,
            concat_axis=0,
            tiled=True,
        ),
    )
    owner_group = expert_ids // group_size
    member = expert_ids % group_size
    slot_place = jnp.take_along_axis(position, owner_group, axis=1)
    flat_slot = owner_group * capacity + slot_place
    grad_gates = back_gate.reshape(slot_total, group_size)[flat_slot, member]
    routed_index = jnp.arange(routed, dtype=jnp.int32)
    earlier = (owner_group[:, :, None] == owner_group[:, None, :]) & (
        routed_index[None, None, :] < routed_index[None, :, None]
    )
    first_seen = jnp.logical_not(jnp.any(earlier, axis=2))
    rows_back = back_in.reshape(slot_total, model_width)[flat_slot]
    grad_tokens = jnp.sum(jnp.where(first_seen[:, :, None], rows_back, 0.0), axis=1).astype(
        jnp.bfloat16
    )
    return (
        grad_tokens,
        grad_gates,
        grad_w_gate.astype(jnp.bfloat16),
        grad_w_up.astype(jnp.bfloat16),
        grad_w_down.astype(jnp.bfloat16),
    )


def solution(mesh):
    in_specs = (
        P(("rep", "node", "local"), None),
        P(("rep", "node", "local"), None),
        P(("rep", "node", "local"), None),
        P(("rep", "node", "local"), None),
        P("node", None, "local"),
        P("node", None, "local"),
        P("node", "local", None),
    )
    out_specs = (
        P(("rep", "node", "local"), None),
        P(("rep", "node", "local"), None),
        P(("rep", "node"), None, "local"),
        P(("rep", "node"), None, "local"),
        P(("rep", "node"), "local", None),
    )
    return jax.shard_map(
        on_device, mesh=mesh, in_specs=in_specs, out_specs=out_specs, check_vma=False
    )
```

profile of v0, /device:TPU:0, one launch (start us, length us, event | category | flops | bytes accessed | tf_op | source)
XLA Modules:
  0.0 776.5 jit_solution(5683085118004299884)
XLA Ops:
  21.7 7.3 all-to-all-start
  44.0 31.2 %all-to-all-done.1 = bf16[8,96,1024]{2,1,0:T(8,128)(2,1)S(1)} async-done(((bf16[8,96,1024]{2,1,0:T(8,128)(2,1)}), bf16[8,96,1024]{2,1,0:T(8,128)(2,1)S(1)}, u32[]{:S(2)}, u32[]{:S(2)}) %all-to-all-start.1) | async-done | bytes 1572896 | tf_op jit(solution)/shard_map/all_to_all | solution.py:143
  90.8 11.8 %scatter_custom_fusion.2 = s32[2688]{0:T(1024)S(1)} fusion(s32[3072]{0:T(1024)S(1)} %bitcast.163, s32[3072]{0:T(1024)S(1)} %reshape.410, s32[]{:T(128)} %constant.153.clone.1), kind=kCustom, calls=%fused_computation.170 | custom fusion | bytes 10756 | tf_op jit(solution)/shard_map/scatter | solution.py:46
  102.6 11.8 %scatter_custom_fusion.3 = f32[2688]{0:T(1024)S(1)} fusion(s32[3072]{0:T(1024)S(1)} %bitcast.164, f32[3072]{0:T(1024)S(1)} %reshape.418, f32[]{:T(128)} %constant.158.clone.1), kind=kCustom, calls=%fused_computation.168 | custom fusion | bytes 10756 | tf_op jit(solution)/shard_map/scatter | solution.py:50
  114.4 11.8 %scatter_custom_fusion.4 = f32[2688]{0:T(1024)S(1)} fusion(s32[3072]{0:T(1024)S(1)} %bitcast.165, f32[3072]{0:T(1024)S(1)} %broadcast.365, f32[]{:T(128)} %constant.158.clone.1), kind=kCustom, calls=%fused_computation.166 | custom fusion | bytes 10756 | tf_op jit(solution)/shard_map/scatter | solution.py:52
  143.5 6.3 copy.130
  149.9 6.3 copy.131
  162.8 433.9 %while.21 = (s32[]{:T(128)}, f32[768,1024]{1,0:T(8,128)}, f32[768,4]{0,1:T(4,128)S(1)}, bf16[2688,384]{1,0:T(8,128)(2,1)}, bf16[2688,384]{1,0:T(8,128)(2,1)}, /*...) while((s32[]{:T(128)}, f32[768,1024]{1,0:T(8,128)}, ...), condition=%wide.region_19.20_spmd, body=%wide.region_15.19_spmd.sunk | while | flops 504514816 | bytes 10794871 | solution.py:90
  184.7 7.0 scatter_fusion.1
  213.7 7.0 scatter_fusion.1
  242.6 7.0 scatter_fusion.1
  271.5 7.0 scatter_fusion.1
  300.4 7.0 scatter_fusion.1
  329.4 7.0 scatter_fusion.1
  358.3 7.0 scatter_fusion.1
  387.2 7.0 scatter_fusion.1
  416.2 7.0 scatter_fusion.1
  445.1 7.0 scatter_fusion.1
  474.0 7.0 scatter_fusion.1
  503.0 7.0 scatter_fusion.1
  531.9 7.0 scatter_fusion.1
  560.8 7.0 scatter_fusion.1
  589.8 7.0 scatter_fusion.1
  603.2 14.1 %pad_maximum_fusion.2 = f32[4,384,1024]{2,1,0:T(8,128)} fusion(f32[1,384,1024]{2,1,0:T(8,128)S(1)} %fusion.31, f32[1,384,1024]{2,1,0:T(8,128)S(1)} %fusion.32, f32[1,384,1024]{2,1,0:T(8,128)S(1)} %fusion.33, f32[1,384,1024]{2,1,0:T(8,128)S(1)} %fusion.34), kind=kLoop, calls=%fused_computation.59 | loop fusion | flops 4718592 | bytes 12582912 | tf_op jit(solution)/shard_map/stack | solution.py:111
  617.6 7.1 gather_fusion.15
  641.5 5.9 all-to-all-start.4
  664.9 8.0 %copy.134 = f32[4,1024,384]{1,0,2:T(4,128)} copy(f32[4,1024,384]{2,1,0:T(8,128)} %pad_maximum_fusion) | data formatting | bytes 12582912 | tf_op jit(solution)/shard_map/stack | solution.py:111
  672.9 8.1 %copy.135 = f32[4,1024,384]{1,0,2:T(4,128)} copy(f32[4,1024,384]{2,1,0:T(8,128)} %pad_maximum_fusion.1) | data formatting | bytes 12582912 | tf_op jit(solution)/shard_map/stack | solution.py:111
  681.0 6.0 all-to-all-start.3
  686.9 35.9 %all-reduce.6 = (bf16[4,1024,384]{1,0,2:T(4,128)(2,1)}, bf16[4,1024,384]{1,0,2:T(4,128)(2,1)}) all-reduce(f32[4,1024,384]{1,0,2:T(4,128)} %copy.134, f32[4,1024,384]{1,0,2:T(4,128)} %copy.135), channel_id=2, replica_groups=mesh['rep'=2,'node'=8,'local'=2] {'local'}, use_global_device_ids=true, to_apply=%region_21.22.clone | all-reduce | flops 3145728 | bytes 18874368
  729.5 9.5 %gather_fusion.6 = f32[1024]{0:T(1024)S(1)} fusion(f32[768,4]{0,1:T(4,128)S(1)} %reshape.266, s32[1024]{0:T(1024)S(1)} %reshape.316), kind=kCustom, calls=%fused_computation.6 | custom fusion | bytes 16384 | tf_op jit(solution)/shard_map/gather | solution.py:182
  739.7 17.0 %all-to-all-done.3 = f32[8,96,1024]{2,1,0:T(8,128)S(1)} async-done(((f32[8,96,1024]{2,1,0:T(8,128)}), f32[8,96,1024]{2,1,0:T(8,128)S(1)}, u32[]{:S(2)}, u32[]{:S(2)}) %all-to-all-start.3) | async-done | bytes 3145760 | tf_op jit(solution)/shard_map/all_to_all | solution.py:163
  (371 shorter events, 421.2 us)
Async XLA Ops:
  7.2 21.9 %copy-start = (bf16[128,1024]{1,0:T(8,128)(2,1)S(1)}, bf16[128,1024]{1,0:T(8,128)(2,1)}, u32[]{:S(2)}) copy-start(bf16[128,1024]{1,0:T(8,128)(2,1)} %param.10) | copy-start | bytes 786436
  7.2 136.4 %all-gather.6.cloned.1.call-start = ((), (), s32[]{:S(2)}) async-start(), calls=%async_computation.7 | async-start | bytes 4718592 | tf_op jit(solution)/shard_map/all_gather | solution.py:151
  11.0 1.4 copy-start.6
  11.1 138.8 %all-gather.8.cloned.1.call-start = ((), (), s32[]{:S(2)}) async-start(), calls=%async_computation.8 | async-start | bytes 4718592 | tf_op jit(solution)/shard_map/all_gather | solution.py:150
  14.8 0.7 copy-start.16
  14.9 0.7 copy-start.15
  21.7 13.8 %all-to-all-start = ((bf16[8,96,4]{1,2,0:T(4,128)(2,1)}), bf16[8,96,4]{1,2,0:T(4,128)(2,1)S(1)}, u32[]{:S(2)}, u32[]{:S(2)}) async-start(bf16[8,96,4]{1,2,0:T(4,128)(2,1)} %select_convert_fusion), calls=%async_computation | async-start | bytes 16384 | tf_op jit(solution)/shard_map/all_to_all | solution.py:144
  35.5 39.7 %all-to-all-start.1 = ((bf16[8,96,1024]{2,1,0:T(8,128)(2,1)}), bf16[8,96,1024]{2,1,0:T(8,128)(2,1)S(1)}, u32[]{:S(2)}, u32[]{:S(2)}) async-start(bf16[8,96,1024]{2,1,0:T(8,128)(2,1)} %bitcast.15), calls=%async_computation.1 | async-start | bytes 3145728 | tf_op jit(solution)/shard_map/all_to_all | solution.py:143
  39.1 1.0 copy-start.2
  39.1 117.0 %all-gather.4.cloned.1.call-start = ((), (), s32[]{:S(2)}) async-start(), calls=%async_computation.6 | async-start | bytes 4718592 | tf_op jit(solution)/shard_map/all_gather | solution.py:152
  75.2 80.9 %all-to-all-start.2 = ((bf16[8,96,1024]{2,1,0:T(8,128)(2,1)}), bf16[8,96,1024]{2,1,0:T(8,128)(2,1)S(1)}, u32[]{:S(2)}, u32[]{:S(2)}) async-start(bf16[8,96,1024]{2,1,0:T(8,128)(2,1)} %bitcast.158), calls=%async_computation.2 | async-start | bytes 3145728 | tf_op jit(solution)/shard_map/all_to_all | solution.py:142
  78.8 687.6 %reduce-scatter.2.cloned.1.call-start = ((), (), s32[]{:S(2)}) async-start(), calls=%async_computation.9 | async-start | bytes 9437184 | tf_op jit(solution)/shard_map/reduce_scatter | solution.py:160
  596.8 2.7 copy-start.3
  596.8 2.7 copy-start.9
  599.5 1.4 copy-start.8
  600.9 1.4 copy-start.7
  617.6 7.8 %copy-start.17 = (u32[32]{0:T(128)S(1)}, u32[32]{0:T(128)}, u32[]{:S(2)}) copy-start(u32[32]{0:T(128)} %constant.234) | copy-start | bytes 388
  641.5 39.5 %all-to-all-start.4 = ((f32[8,96,4]{1,2,0:T(4,128)}), f32[8,96,4]{1,2,0:T(4,128)S(1)}, u32[]{:S(2)}, u32[]{:S(2)}) async-start(f32[8,96,4]{1,2,0:T(4,128)} %copy.132), calls=%async_computation.4 | async-start | bytes 32768 | tf_op jit(solution)/shard_map/all_to_all | solution.py:170
  647.4 2.8 copy-start.5
  647.4 2.8 copy-start.13
  650.2 1.6 copy-start.4
  650.2 2.0 copy-start.12
  653.2 1.4 copy-start.11
  655.7 1.4 copy-start.10
  681.0 75.7 %all-to-all-start.3 = ((f32[8,96,1024]{2,1,0:T(8,128)}), f32[8,96,1024]{2,1,0:T(8,128)S(1)}, u32[]{:S(2)}, u32[]{:S(2)}) async-start(f32[8,96,1024]{2,1,0:T(8,128)} %bitcast.157), calls=%async_computation.3 | async-start | bytes 6291456 | tf_op jit(solution)/shard_map/all_to_all | solution.py:163
  724.8 2.5 copy-start.14
  762.1 7.6 copy-start.1
Sparse Core Ops, SparseCore 0:
  11.2 14.8 all-gather.5
  27.6 13.2 all-gather.7
  42.5 13.2 all-gather.3
  617.4 15.8 reduce-scatter.1
where the time goes:
time: 785 us; the launch traced here: 776 us
  other arithmetic  239 us (30%)
  local copies, waits for them, and re-layouts  216 us (28%)
  matrix products  155 us (20%)
  waiting for transfers between devices  51.8 us (7%)
  blocking collectives  35.9 us (5%)
  loops' own time  30.1 us (4%)
  starting transfers between devices  26.5 us (3%)
  between operations  22.6 us (3%)
    scatter-add x15, other arithmetic, advance(): gate_state = gate_state.at[rows, expert].add(present * results[1])  105 us
    scatter-add x15, other arithmetic, advance(): input_state = input_state.at[rows].add(results[0])  85.5 us
    unnamed x1, blocking collectives  35.9 us
    dot_general x15, matrix products, block_rows(): pre_gate = jnp.dot(rows_in, gate_weight, preferred_element_type=jnp.float32)  35.3 us
    dot_general x15, matrix products, block_rows(): jnp.dot(grad_pre_up, up_weight.T, preferred_element_type=jnp.float32)  34.8 us
    all_to_all x1, waiting for transfers between devices, on_device(): lax.all_to_all(send_grad, 'node', split_axis=0, concat_axis=0, tiled=True)  31.2 us
    another operation x1, loops' own time, process(): final = lax.fori_loop(0, block_limit, advance, initial)  30.1 us
    dot_general x15, matrix products, block_rows(): jnp.dot(rows_grad, down_weight.T, preferred_element_type=jnp.float32)  23.8 us
  transfers between devices with their start and end apart: 9, of which 3 were waited for; matrix products, arithmetic and copies ran while one was open for 22% of the time, Pallas kernels for 0%

commit v1 on v0

--- a/solution.py
+++ b/solution.py
@@ -1,9 +1,13 @@
 import jax
 import jax.numpy as jnp
 from jax import lax
+from jax.experimental import pallas as pl
+from jax.experimental.pallas import tpu as pltpu
 from jax.sharding import PartitionSpec as P
 
 LIMIT = 4
+LANES = 128
+BLOCK = 256
 
 
 def silu_terms(pre_gate):
@@ -111,7 +115,7 @@
     return (final[0], final[1], (jnp.stack(gate_list), jnp.stack(up_list), jnp.stack(down_list)))
 
 
-def on_device(tokens, grad_out, expert_ids, gate_values, w_gate, w_up, w_down):
+def routed_on_device(tokens, grad_out, expert_ids, gate_values, w_gate, w_up, w_down):
     token_count, model_width = tokens.shape
     group_size = w_gate.shape[0]
     routed = expert_ids.shape[1]
@@ -198,6 +202,144 @@
     )
 
 
+def contract(left, right, left_dim, right_dim):
+    return lax.dot_general(
+        left, right, (((left_dim,), (right_dim,)), ((), ())), preferred_element_type=jnp.float32
+    )
+
+
+def dense_kernel(
+    x_ref,
+    g_ref,
+    t_ref,
+    gate_ref,
+    up_ref,
+    down_ref,
+    pick_ref,
+    back_ref,
+    dgate_ref,
+    dup_ref,
+    ddown_ref,
+    acc_gate,
+    acc_up,
+    acc_down,
+):
+    step = pl.program_id(0)
+    width = x_ref.shape[1]
+    rows, grads = x_ref[...], g_ref[...]
+    pre_gate = contract(rows, gate_ref[...], 1, 1)
+    pre_up = contract(rows, up_ref[...], 1, 1)
+    back_hidden = contract(grads, down_ref[...], 1, 1)
+    gate = contract(t_ref[...], pick_ref[...], 1, 0)
+    activated, slope = silu_terms(pre_gate)
+    hidden = activated * pre_up
+    product = back_hidden * hidden
+    high = product.astype(jnp.bfloat16)
+    low = (product - high.astype(jnp.float32)).astype(jnp.bfloat16)
+    scaled = gate * back_hidden
+    grad_gate = (scaled * pre_up * slope).astype(jnp.bfloat16)
+    grad_up = (scaled * activated).astype(jnp.bfloat16)
+    weighted = (gate * hidden).astype(jnp.bfloat16)
+    back_ref[:, :width] = contract(grad_gate, gate_ref[...], 1, 0) + contract(
+        grad_up, up_ref[...], 1, 0
+    )
+    back_ref[:, width:] = contract(high, pick_ref[...], 1, 1) + contract(low, pick_ref[...], 1, 1)
+    sums = (
+        (acc_gate, dgate_ref, contract(grad_gate, rows, 0, 0)),
+        (acc_up, dup_ref, contract(grad_up, rows, 0, 0)),
+        (acc_down, ddown_ref, contract(weighted, grads, 0, 0)),
+    )
+
+    @pl.when(step == 0)
+    def _():
+        for acc, _, new in sums:
+            acc[...] = new
+
+    @pl.when(step > 0)
+    def _():
+        for acc, _, new in sums:
+            acc[...] += new
+
+    @pl.when(step == pl.num_programs(0) - 1)
+    def _():
+        for acc, out, _ in sums:
+            out[...] = acc[...].astype(jnp.bfloat16)
+
+
+def dense_rows(payload, gate, up, down, pick):
+    total = payload.shape[0]
+    units, width = down.shape
+    tail = 2 * width // LANES
+    whole = lambda shape: pl.BlockSpec(shape, lambda i: (0, 0))
+    return pl.pallas_call(
+        dense_kernel,
+        grid=(total // BLOCK,),
+        in_specs=[
+            pl.BlockSpec((BLOCK, width), lambda i: (i, 0)),
+            pl.BlockSpec((BLOCK, width), lambda i: (i, 1)),
+            pl.BlockSpec((BLOCK, LANES), lambda i: (i, tail)),
+            whole(down.shape),
+            whole(down.shape),
+            whole(down.shape),
+            whole(pick.shape),
+        ],
+        out_specs=[
+            pl.BlockSpec((BLOCK, width + LANES), lambda i: (i, 0)),
+            whole(down.shape),
+            whole(down.shape),
+            whole(down.shape),
+        ],
+        out_shape=[
+            jax.ShapeDtypeStruct((total, width + LANES), jnp.float32),
+            jax.ShapeDtypeStruct(down.shape, jnp.bfloat16),
+            jax.ShapeDtypeStruct(down.shape, jnp.bfloat16),
+            jax.ShapeDtypeStruct(down.shape, jnp.bfloat16),
+        ],
+        scratch_shapes=[
+            pltpu.VMEM(down.shape, jnp.float32),
+            pltpu.VMEM(down.shape, jnp.float32),
+            pltpu.VMEM(down.shape, jnp.float32),
+        ],
+        compiler_params=pltpu.CompilerParams(vmem_limit_bytes=58 * 1024 * 1024),
+        cost_estimate=pl.CostEstimate(
+            flops=16 * total * width * units,
+            bytes_accessed=total * width * 8 + width * units * 12,
+            transcendentals=total * units,
+        ),
+    )(payload, payload, payload, gate, up, down, pick)
+
+
+def on_device(tokens, grad_out, expert_ids, gate_values, w_gate, w_up, w_down):
+    node_count = lax.axis_size("node")
+    group_size, width, half = w_gate.shape
+    if node_count > 2 * LIMIT or group_size * node_count > LANES:
+        return routed_on_device(tokens, grad_out, expert_ids, gate_values, w_gate, w_up, w_down)
+    token_count = tokens.shape[0]
+    units = group_size * half
+    experts = jnp.arange(LANES, dtype=jnp.int32)
+    hits = expert_ids[:, :, None] == experts[None, None, :]
+    table = jnp.sum(jnp.where(hits, gate_values.astype(jnp.float32)[:, :, None], 0.0), axis=1)
+    payload = jnp.concatenate([tokens, grad_out, table.astype(jnp.bfloat16)], axis=1)
+    payload = lax.all_gather(payload, ("node", "local"), axis=0, tiled=True)
+    gate = w_gate.transpose(0, 2, 1).reshape(units, width)
+    up = w_up.transpose(0, 2, 1).reshape(units, width)
+    down = w_down.reshape(units, width)
+    mine = lax.axis_index("node") * group_size + jnp.arange(units, dtype=jnp.int32) // half
+    pick = (experts[:, None] == mine[None, :]).astype(jnp.bfloat16)
+    back, grad_gate, grad_up, grad_down = dense_rows(payload, gate, up, down, pick)
+    back = lax.psum_scatter(back, ("node", "local"), scatter_dimension=0, tiled=True)
+    grad_tokens = back[:, :width].astype(jnp.bfloat16)
+    grad_table = back[:, width:]
+    grad_gates = jnp.sum(jnp.where(hits, grad_table[:, None, :], 0.0), axis=2)
+    return (
+        grad_tokens,
+        grad_gates,
+        grad_gate.reshape(group_size, half, width).transpose(0, 2, 1),
+        grad_up.reshape(group_size, half, width).transpose(0, 2, 1),
+        grad_down.reshape(group_size, half, width),
+    )
+
+
 def solution(mesh):
     in_specs = (
         P(("rep", "node", "local"), None),

time: 785 us -> 258 us (0.33); the launches traced: 776 us -> 258 us
  other arithmetic: 239 us -> 3.32 us
  local copies, waits for them, and re-layouts: 216 us -> 4.85 us
  matrix products: 155 us -> 0 us
  waiting for transfers between devices: 51.8 us -> 190 us
  Pallas kernels: 0 us -> 45.3 us
  blocking collectives: 35.9 us -> 0 us
  loops' own time: 30.1 us -> 0 us
  starting transfers between devices: 26.5 us -> 0.08 us
  between operations: 22.6 us -> 14.1 us
    scatter-add x30 -> x0, other arithmetic: 190 us -> none  [the longest x15 105 us: advance(): gate_state = gate_state.at[rows, expert].add(present * results[1])]
    dot_general x87 -> x0, matrix products: 155 us -> none  [the longest x15 35.3 us: block_rows(): pre_gate = jnp.dot(rows_in, gate_weight, preferred_element_type=jnp.float32)]
    reduce_scatter x1, waiting for transfers between devices: 0.01 us -> 110 us  [on_device(): lax.psum_scatter(back, ('node', 'local'), scatter_dimension=0, tiled=True)]
    gather x48 -> x0, local copies, waits for them, and re-layouts: 109 us -> none  [the longest x15 23.5 us: advance(): rows_grad[rows]]
    all_gather x3 -> x1, waiting for transfers between devices: 0.01 us -> 80.3 us  [on_device(): payload = lax.all_gather(payload, ('node', 'local'), axis=0, tiled=True)]
    all_to_all x5 -> x0, waiting for transfers between devices: 51 us -> none  [the longest x1 31.2 us: on_device(): lax.all_to_all(send_grad, 'node', split_axis=0, concat_axis=0, tiled=True)]
    pallas_call x0 -> x1, Pallas kernels: none -> 45.3 us  [dense_rows(): pl.pallas_call(dense_kernel, grid=(total // BLOCK,), in_specs=[pl.BlockSp...]
    unnamed x1 -> x0, blocking collectives: 35.9 us -> none
  transfers between devices with their start and end apart: 9 -> 2, of which waited for: 3 -> 2; matrix products, arithmetic and copies ran while one was open for 22% -> 0% of each run, Pallas kernels for 0% -> 0%
where the time goes in v1:
time: 258 us
  waiting for transfers between devices  190 us (74%)
  Pallas kernels  45.3 us (18%)
  between operations  14.1 us (5%)
  local copies, waits for them, and re-layouts  4.85 us (2%)
  other arithmetic  3.32 us (1%)
    reduce_scatter x1, waiting for transfers between devices, on_device(): lax.psum_scatter(back, ('node', 'local'), scatter_dimension=0, tiled=True)  110 us
    all_gather x1, waiting for transfers between devices, on_device(): payload = lax.all_gather(payload, ('node', 'local'), axis=0, tiled=True)  80.3 us
    pallas_call x1, Pallas kernels, dense_rows(): pl.pallas_call(dense_kernel, grid=(total // BLOCK,), in_specs=[pl.BlockSp...  45.3 us
  transfers between devices with their start and end apart: 2, of which 2 were waited for; matrix products, arithmetic and copies ran while one was open for 0% of the time, Pallas kernels for 0%

profile of v1, /device:TPU:0, one launch (start us, length us, event | category | flops | bytes accessed | tf_op | source)
XLA Modules:
  0.0 257.6 jit_solution(3118274462609883636)
XLA Ops:
  7.2 0.0 all-gather.2.cloned.1.call-start
  7.2 0.8 copy.14
  8.0 0.8 copy.15
  8.8 0.4 select_reduce_fusion.1
  9.1 1.9 pad_maximum_fusion
  11.0 0.0 all-gather.2.cloned.1.call-update
  11.0 0.0 reduce-scatter.2.cloned.1.call-start
  11.1 0.7 fusion.pick_ref
  11.8 80.3 %all-gather.2.cloned.1.call-done.x_ref.g_ref.t_ref = bf16[2048,2176]{1,0:T(8,128)(2,1)} async-done(((bf16[128,2176]{1,0:T(8,128)(2,1)}), bf16[2048,2176]{1,0:T(8,128)(2,1)}) %all-gather.2.cloned.1.call-update) | async-done | bytes 8912912 | tf_op jit(solution)/shard_map/all_gather | solution.py:323
  92.1 45.3 %shard_map.110 = (f32[2048,1152]{1,0:T(8,128)}, bf16[768,1024]{1,0:T(8,128)(2,1)}, bf16[768,1024]{1,0:T(8,128)(2,1)}, bf16[768,1024]{1,0:T(8,128)(2,1)}) custom-call(bf16[2048,2176]{1,0:T(8,128)(2,1)} %all-gather.2.cloned.1.call-done.x_ref.g_ref.t_ref, bf16[2048,2176]{1,0:T(8,128)(2,1)} %all-gather.2.cloned.1.call-done.x_ref.g_ref.t_ref, ...), custom_call_target="tpu_custom_call" | custom-call | flops 25769803776 | bytes 26214400 | tf_op jit(solution)/shard_map/pallas_call | solution.py:274
  137.4 0.0 reduce-scatter.2.cloned.1.call-update
  137.5 109.7 %reduce-scatter.2.cloned.1.call-done = f32[128,1152]{1,0:T(8,128)} async-done(((f32[2048,1152]{1,0:T(8,128)}), f32[128,1152]{1,0:T(8,128)}) %reduce-scatter.2.cloned.1.call-update) | async-done | bytes 589840 | tf_op jit(solution)/shard_map/reduce_scatter | solution.py:330
  247.1 0.8 slice.10
  248.0 0.4 select_reduce_fusion
  248.3 0.7 copy.16
  249.0 1.8 slice.12
  (1 shorter events, 0.0 us)
Async XLA Ops:
  7.2 84.9 %all-gather.2.cloned.1.call-start = ((), (), s32[]{:S(2)}) async-start(), calls=%async_computation.1 | async-start | bytes 9469952 | tf_op jit(solution)/shard_map/all_gather | solution.py:323
  11.0 236.1 %reduce-scatter.2.cloned.1.call-start = ((), (), s32[]{:S(2)}) async-start(), calls=%async_computation.2 | async-start | bytes 10027008 | tf_op jit(solution)/shard_map/reduce_scatter | solution.py:330
Sparse Core Ops, SparseCore 0:
  11.2 80.8 all-gather.1
  137.6 109.4 reduce-scatter.1

commit v2 on v0

--- a/solution.py
+++ b/solution.py
@@ -1,9 +1,15 @@
+import functools
+
 import jax
 import jax.numpy as jnp
 from jax import lax
+from jax.experimental import pallas as pl
+from jax.experimental.pallas import tpu as pltpu
 from jax.sharding import PartitionSpec as P
 
 LIMIT = 4
+LANES = 128
+MESH = pl.DeviceIdType.MESH
 
 
 def silu_terms(pre_gate):
@@ -111,7 +117,7 @@
     return (final[0], final[1], (jnp.stack(gate_list), jnp.stack(up_list), jnp.stack(down_list)))
 
 
-def on_device(tokens, grad_out, expert_ids, gate_values, w_gate, w_up, w_down):
+def routed_on_device(tokens, grad_out, expert_ids, gate_values, w_gate, w_up, w_down):
     token_count, model_width = tokens.shape
     group_size = w_gate.shape[0]
     routed = expert_ids.shape[1]
@@ -198,6 +204,241 @@
     )
 
 
+def contract(left, right, left_dim, right_dim):
+    return lax.dot_general(
+        left, right, (((left_dim,), (right_dim,)), ((), ())), preferred_element_type=jnp.float32
+    )
+
+
+def fused_kernel(
+    node_count,
+    payload_ref,
+    gate_ref,
+    up_ref,
+    down_ref,
+    pick_ref,
+    tokens_ref,
+    table_ref,
+    dgate_ref,
+    dup_ref,
+    ddown_ref,
+    rows_ref,
+    acc_gate,
+    acc_up,
+    acc_down,
+    keep,
+    share_out,
+    share_in,
+    back_out,
+    back_in,
+    row_send,
+    row_recv,
+    pair_send,
+    pair_recv,
+    share_send,
+    share_recv,
+    back_send,
+    back_recv,
+):
+    count = payload_ref.shape[0]
+    width = gate_ref.shape[1]
+    me = lax.axis_index("node")
+    partner = {"local": 1 - lax.axis_index("local")}
+
+    def ahead(s):
+        return {"node": lax.rem(me + s, node_count)}
+
+    def behind(s):
+        return {"node": lax.rem(me + node_count - s, node_count)}
+
+    def row_copy(s):
+        return pltpu.make_async_remote_copy(
+            src_ref=payload_ref,
+            dst_ref=rows_ref.at[s, pl.ds(0, count)],
+            send_sem=row_send.at[s],
+            recv_sem=row_recv.at[s],
+            device_id=ahead(s),
+            device_id_type=MESH,
+        )
+
+    def pair_copy(s):
+        return pltpu.make_async_remote_copy(
+            src_ref=rows_ref.at[s, pl.ds(0, count)],
+            dst_ref=rows_ref.at[s, pl.ds(count, count)],
+            send_sem=pair_send.at[s],
+            recv_sem=pair_recv.at[s],
+            device_id=partner,
+            device_id_type=MESH,
+        )
+
+    def share_copy(s):
+        return pltpu.make_async_remote_copy(
+            src_ref=share_out.at[s],
+            dst_ref=share_in.at[s],
+            send_sem=share_send.at[s],
+            recv_sem=share_recv.at[s],
+            device_id=partner,
+            device_id_type=MESH,
+        )
+
+    def back_copy(s):
+        return pltpu.make_async_remote_copy(
+            src_ref=back_out.at[s],
+            dst_ref=back_in.at[s],
+            send_sem=back_send.at[s],
+            recv_sem=back_recv.at[s],
+            device_id=behind(s),
+            device_id_type=MESH,
+        )
+
+    barrier = pltpu.get_barrier_semaphore()
+    for s in range(1, node_count):
+        pl.semaphore_signal(barrier, inc=1, device_id=ahead(s), device_id_type=MESH)
+    pl.semaphore_signal(barrier, inc=1, device_id=partner, device_id_type=MESH)
+    pl.semaphore_wait(barrier, node_count)
+
+    for s in range(1, node_count):
+        row_copy(s).start()
+    rows_ref[0, :count, :] = payload_ref[...]
+    pair_copy(0).start()
+    for acc in (acc_gate, acc_up, acc_down):
+        acc[...] = jnp.zeros_like(acc)
+
+    def finish(s):
+        share_copy(s).wait_recv()
+        return keep[lax.rem(s, 2)] + share_in[s].astype(jnp.float32)
+
+    def send_back(s):
+        back_out[s] = finish(s).astype(jnp.bfloat16)
+        back_copy(s).start()
+
+    def advance(s, carry):
+        @pl.when(s < node_count - 1)
+        def _():
+            row_copy(s + 1).wait_recv()
+            pair_copy(s + 1).start()
+
+        pair_copy(s).wait_recv()
+        rows = rows_ref[s, :, :width]
+        grads = rows_ref[s, :, width : 2 * width]
+        pre_gate = contract(rows, gate_ref[...], 1, 1)
+        pre_up = contract(rows, up_ref[...], 1, 1)
+        back_hidden = contract(grads, down_ref[...], 1, 1)
+        gate = contract(rows_ref[s, :, 2 * width :], pick_ref[...], 1, 0)
+        activated, slope = silu_terms(pre_gate)
+        hidden = activated * pre_up
+        product = back_hidden * hidden
+        high = product.astype(jnp.bfloat16)
+        low = (product - high.astype(jnp.float32)).astype(jnp.bfloat16)
+        scaled = gate * back_hidden
+        grad_gate = (scaled * pre_up * slope).astype(jnp.bfloat16)
+        grad_up = (scaled * activated).astype(jnp.bfloat16)
+        weighted = (gate * hidden).astype(jnp.bfloat16)
+        back = contract(grad_gate, gate_ref[...], 1, 0) + contract(grad_up, up_ref[...], 1, 0)
+        sums = contract(high, pick_ref[...], 1, 1) + contract(low, pick_ref[...], 1, 1)
+        share_out[s, :, :width] = back[count:].astype(jnp.bfloat16)
+        share_out[s, :, width:] = sums[count:].astype(jnp.bfloat16)
+        share_copy(s).start()
+        keep[lax.rem(s, 2), :, :width] = back[:count]
+        keep[lax.rem(s, 2), :, width:] = sums[:count]
+
+        @pl.when(s == 1)
+        def _():
+            keep[2] = finish(0)
+
+        @pl.when(s > 1)
+        def _():
+            send_back(s - 1)
+
+        acc_gate[...] += contract(grad_gate, rows, 0, 0)
+        acc_up[...] += contract(grad_up, rows, 0, 0)
+        acc_down[...] += contract(weighted, grads, 0, 0)
+        return carry
+
+    lax.fori_loop(0, node_count, advance, 0)
+    send_back(node_count - 1)
+    dgate_ref[...] = acc_gate[...].astype(jnp.bfloat16)
+    dup_ref[...] = acc_up[...].astype(jnp.bfloat16)
+    ddown_ref[...] = acc_down[...].astype(jnp.bfloat16)
+    for s in range(1, node_count):
+        back_copy(s).wait_recv()
+        keep[2] += back_in[s].astype(jnp.float32)
+    tokens_ref[...] = keep[2, :, :width].astype(jnp.bfloat16)
+    table_ref[...] = keep[2, :, width:]
+    for s in range(node_count):
+        pair_copy(s).wait_send()
+        share_copy(s).wait_send()
+        if s > 0:
+            row_copy(s).wait_send()
+            back_copy(s).wait_send()
+
+
+def fused(node_count, payload, gate, up, down, pick):
+    count = payload.shape[0]
+    units, width = down.shape
+    wide = width + LANES
+    vmem = pl.BlockSpec(memory_space=pltpu.VMEM)
+    total = 2 * count * node_count
+    return pl.pallas_call(
+        functools.partial(fused_kernel, node_count),
+        in_specs=[vmem] * 5,
+        out_specs=[vmem] * 5,
+        out_shape=[
+            jax.ShapeDtypeStruct((count, width), jnp.bfloat16),
+            jax.ShapeDtypeStruct((count, LANES), jnp.float32),
+            jax.ShapeDtypeStruct(down.shape, jnp.bfloat16),
+            jax.ShapeDtypeStruct(down.shape, jnp.bfloat16),
+            jax.ShapeDtypeStruct(down.shape, jnp.bfloat16),
+        ],
+        scratch_shapes=[
+            pltpu.VMEM((node_count, 2 * count, payload.shape[1]), jnp.bfloat16),
+            pltpu.VMEM(down.shape, jnp.float32),
+            pltpu.VMEM(down.shape, jnp.float32),
+            pltpu.VMEM(down.shape, jnp.float32),
+            pltpu.VMEM((3, count, wide), jnp.float32),
+        ]
+        + [pltpu.VMEM((node_count, count, wide), jnp.bfloat16)] * 4
+        + [pltpu.SemaphoreType.DMA((node_count,))] * 8,
+        compiler_params=pltpu.CompilerParams(
+            collective_id=0, has_side_effects=True, vmem_limit_bytes=60 * 1024 * 1024
+        ),
+        cost_estimate=pl.CostEstimate(
+            flops=16 * total * width * units,
+            bytes_accessed=width * units * 12,
+            transcendentals=total * units,
+        ),
+    )(payload, gate, up, down, pick)
+
+
+def on_device(tokens, grad_out, expert_ids, gate_values, w_gate, w_up, w_down):
+    node_count = lax.axis_size("node")
+    group_size, width, half = w_gate.shape
+    if node_count > 2 * LIMIT or group_size * node_count > LANES:
+        return routed_on_device(tokens, grad_out, expert_ids, gate_values, w_gate, w_up, w_down)
+    token_count = tokens.shape[0]
+    units = group_size * half
+    experts = jnp.arange(LANES, dtype=jnp.int32)
+    hits = expert_ids[:, :, None] == experts[None, None, :]
+    table = jnp.sum(jnp.where(hits, gate_values.astype(jnp.float32)[:, :, None], 0.0), axis=1)
+    payload = jnp.concatenate([tokens, grad_out, table.astype(jnp.bfloat16)], axis=1)
+    gate = w_gate.transpose(0, 2, 1).reshape(units, width)
+    up = w_up.transpose(0, 2, 1).reshape(units, width)
+    down = w_down.reshape(units, width)
+    mine = lax.axis_index("node") * group_size + jnp.arange(units, dtype=jnp.int32) // half
+    pick = (experts[:, None] == mine[None, :]).astype(jnp.bfloat16)
+    grad_tokens, grad_table, grad_gate, grad_up, grad_down = fused(
+        node_count, payload, gate, up, down, pick
+    )
+    grad_gates = jnp.sum(jnp.where(hits, grad_table[:, None, :], 0.0), axis=2)
+    return (
+        grad_tokens,
+        grad_gates,
+        grad_gate.reshape(group_size, half, width).transpose(0, 2, 1),
+        grad_up.reshape(group_size, half, width).transpose(0, 2, 1),
+        grad_down.reshape(group_size, half, width),
+    )
+
+
 def solution(mesh):
     in_specs = (
         P(("rep", "node", "local"), None),

time: 785 us -> 191 us (0.24); the launches traced: 776 us -> 191 us
  other arithmetic: 239 us -> 4.17 us
  local copies, waits for them, and re-layouts: 216 us -> 9.81 us
  Pallas kernels: 0 us -> 176 us
  matrix products: 155 us -> 0 us
  waiting for transfers between devices: 51.8 us -> 0 us
  blocking collectives: 35.9 us -> 0 us
  loops' own time: 30.1 us -> 0 us
  starting transfers between devices: 26.5 us -> 0 us
  between operations: 22.6 us -> 0.66 us
    scatter-add x30 -> x0, other arithmetic: 190 us -> none  [the longest x15 105 us: advance(): gate_state = gate_state.at[rows, expert].add(present * results[1])]
    pallas_call x0 -> x1, Pallas kernels: none -> 176 us  [fused(): pl.pallas_call(functools.partial(fused_kernel, node_count), in_specs=[vme...]
    dot_general x87 -> x0, matrix products: 155 us -> none  [the longest x15 35.3 us: block_rows(): pre_gate = jnp.dot(rows_in, gate_weight, preferred_element_type=jnp.float32)]
    gather x48 -> x0, local copies, waits for them, and re-layouts: 109 us -> none  [the longest x15 23.5 us: advance(): rows_grad[rows]]
    all_to_all x5 -> x0, waiting for transfers between devices: 51 us -> none  [the longest x1 31.2 us: on_device(): lax.all_to_all(send_grad, 'node', split_axis=0, concat_axis=0, tiled=True)]
    unnamed x1 -> x0, blocking collectives: 35.9 us -> none
    scatter x3 -> x0, local copies, waits for them, and re-layouts: 35.4 us -> none  [the longest x1 11.8 us: process(): slot_gate = jnp.zeros(buffer_rows, jnp.float32).at[target].set(rows_gate....]
    another operation x1 -> x0, loops' own time: 30.1 us -> none  [process(): final = lax.fori_loop(0, block_limit, advance, initial)]
  transfers between devices with their start and end apart: 9 -> 0, of which waited for: 3 -> 0; matrix products, arithmetic and copies ran while one was open for 22% -> 0% of each run, Pallas kernels for 0% -> 0%
where the time goes in v2:
time: 191 us
  Pallas kernels  176 us (92%)
  local copies, waits for them, and re-layouts  9.81 us (5%)
  other arithmetic  4.17 us (2%)
    pallas_call x1, Pallas kernels, fused(): pl.pallas_call(functools.partial(fused_kernel, node_count), in_specs=[vme...  176 us
    unnamed x10, local copies, waits for them, and re-layouts  9.03 us

profile of v2, /device:TPU:0, one launch (start us, length us, event | category | flops | bytes accessed | tf_op | source)
XLA Modules:
  0.0 191.1 jit_solution(14109293535132598406)
XLA Ops:
  0.7 0.8 copy.14
  1.4 0.8 copy.15
  2.2 0.4 select_reduce_fusion.1
  2.6 0.7 fusion.pick_ref
  3.3 1.9 pad_maximum_fusion.payload_ref
  5.2 176.5 %shard_map.110 = (bf16[128,1024]{1,0:T(8,128)(2,1)}, f32[128,128]{1,0:T(8,128)}, bf16[768,1024]{1,0:T(8,128)(2,1)}, bf16[768,1024]{1,0:T(8,128)(2,1)}, bf16[768,1024]{1,0:T(8,128)(2,1)}) custom-call(bf16[128,2176]{1,0:T(8,128)(2,1)} %pad_maximum_fusion.payload_ref, bf16[768,1024]{1,0:T(8,128)(2,1)} %bitcast.17, bf16[768,1024]{1,0:T(8,128)(2,1)} %bitcast.18, ...), custom_call_target="tpu_custom_call" | custom-call | flops 25769803776 | bytes 9437184 | tf_op jit(solution)/shard_map/pallas_call | solution.py:382
  181.7 1.2 select_reduce_fusion
  182.9 0.7 copy.16
  183.5 1.7 copy.21
  185.2 0.0 copy-start.1
  185.2 2.8 %copy.22 = bf16[4,1024,192]{1,2,0:T(8,128)(2,1)} copy(bf16[4,1024,192]{1,2,0:T(8,128)(2,1)} %bitcast.16) | data formatting | bytes 3145728
  188.0 0.0 copy-done.1
  188.0 0.0 copy-start
  188.0 1.1 copy.23
  189.1 0.8 copy-done
  190.0 1.1 copy.24
  (1 shorter events, 0.0 us)
Async XLA Ops:
  185.2 2.8 %copy-start.1 = (bf16[768,1024]{1,0:T(8,128)(2,1)S(1)}, bf16[768,1024]{1,0:T(8,128)(2,1)}, u32[]{:S(2)}) copy-start(bf16[768,1024]{1,0:T(8,128)(2,1)} %get-tuple-element.13) | copy-start | bytes 4718596
  188.0 2.0 %copy-start = (bf16[768,1024]{1,0:T(8,128)(2,1)S(1)}, bf16[768,1024]{1,0:T(8,128)(2,1)}, u32[]{:S(2)}) copy-start(bf16[768,1024]{1,0:T(8,128)(2,1)} %get-tuple-element.14) | copy-start | bytes 4718596

commit v3 on v2

--- a/solution.py
+++ b/solution.py
@@ -229,37 +229,63 @@
     keep,
     share_out,
     share_in,
-    back_out,
-    back_in,
-    row_send,
-    row_recv,
+    side_out,
+    side_in,
+    line_out,
+    line_in,
+    line_send,
+    line_recv,
+    side_send,
+    side_recv,
     pair_send,
     pair_recv,
     share_send,
     share_recv,
-    back_send,
-    back_recv,
+    side_back_send,
+    side_back_recv,
+    line_back_send,
+    line_back_recv,
 ):
     count = payload_ref.shape[0]
     width = gate_ref.shape[1]
     me = lax.axis_index("node")
+    length = node_count // 2
+    place, side = me // 2, lax.rem(me, 2)
     partner = {"local": 1 - lax.axis_index("local")}
-
-    def ahead(s):
-        return {"node": lax.rem(me + s, node_count)}
-
-    def behind(s):
-        return {"node": lax.rem(me + node_count - s, node_count)}
-
-    def row_copy(s):
+    across = {"node": 2 * place + 1 - side}
+
+    def ahead(k):
+        return {"node": 2 * lax.rem(place + k, length) + side}
+
+    def behind(k):
+        return {"node": 2 * lax.rem(place + length - k, length) + side}
+
+    def remote(source, target, send_sem, recv_sem, device):
         return pltpu.make_async_remote_copy(
-            src_ref=payload_ref,
-            dst_ref=rows_ref.at[s, pl.ds(0, count)],
-            send_sem=row_send.at[s],
-            recv_sem=row_recv.at[s],
-            device_id=ahead(s),
+            src_ref=source,
+            dst_ref=target,
+            send_sem=send_sem,
+            recv_sem=recv_sem,
+            device_id=device,
             device_id_type=MESH,
         )
+
+    def line_copy(k):
+        target = rows_ref.at[2 * k, pl.ds(0, count)]
+        return remote(payload_ref, target, line_send.at[k], line_recv.at[k], ahead(k))
+
+    def side_copy(k):
+        source = rows_ref.at[2 * k, pl.ds(0, count)]
+        target = rows_ref.at[2 * k + 1, pl.ds(0, count)]
+        return remote(source, target, side_send.at[k], side_recv.at[k], across)
+
+    def side_back(k):
+        sems = side_back_send.at[k], side_back_recv.at[k]
+        return remote(side_out.at[k], side_in.at[k], *sems, across)
+
+    def line_back(k):
+        sems = line_back_send.at[k], line_back_recv.at[k]
+        return remote(line_out.at[k], line_in.at[k], *sems, behind(k))
 
     def pair_copy(s):
         return pltpu.make_async_remote_copy(
@@ -281,43 +307,52 @@
             device_id_type=MESH,
         )
 
-    def back_copy(s):
-        return pltpu.make_async_remote_copy(
-            src_ref=back_out.at[s],
-            dst_ref=back_in.at[s],
-            send_sem=back_send.at[s],
-            recv_sem=back_recv.at[s],
-            device_id=behind(s),
-            device_id_type=MESH,
-        )
-
     barrier = pltpu.get_barrier_semaphore()
-    for s in range(1, node_count):
-        pl.semaphore_signal(barrier, inc=1, device_id=ahead(s), device_id_type=MESH)
+    for k in range(1, length):
+        pl.semaphore_signal(barrier, inc=1, device_id=ahead(k), device_id_type=MESH)
+    pl.semaphore_signal(barrier, inc=1, device_id=across, device_id_type=MESH)
     pl.semaphore_signal(barrier, inc=1, device_id=partner, device_id_type=MESH)
-    pl.semaphore_wait(barrier, node_count)
-
-    for s in range(1, node_count):
-        row_copy(s).start()
+    pl.semaphore_wait(barrier, length + 1)
+
+    for k in range(1, length):
+        line_copy(k).start()
     rows_ref[0, :count, :] = payload_ref[...]
+    side_copy(0).start()
     pair_copy(0).start()
     for acc in (acc_gate, acc_up, acc_down):
         acc[...] = jnp.zeros_like(acc)
 
     def finish(s):
         share_copy(s).wait_recv()
-        return keep[lax.rem(s, 2)] + share_in[s].astype(jnp.float32)
-
-    def send_back(s):
-        back_out[s] = finish(s).astype(jnp.bfloat16)
-        back_copy(s).start()
+        k = s // 2
+        part = share_in[s].astype(jnp.float32)
+
+        @pl.when(lax.rem(s, 2) == 0)
+        def _():
+            keep[k] += part
+
+        @pl.when(lax.rem(s, 2) == 1)
+        def _():
+            side_out[k] = (keep[length] + part).astype(jnp.bfloat16)
+            side_back(k).start()
+
+    def send_back(k):
+        side_back(k).wait_recv()
+        whole = keep[k] + side_in[k].astype(jnp.float32)
+
+        @pl.when(k == 0)
+        def _():
+            keep[0] = whole
+
+        @pl.when(k > 0)
+        def _():
+            line_out[k] = whole.astype(jnp.bfloat16)
+            line_back(k).start()
 
     def advance(s, carry):
-        @pl.when(s < node_count - 1)
-        def _():
-            row_copy(s + 1).wait_recv()
-            pair_copy(s + 1).start()
-
+        k = s // 2
+        even = lax.rem(s, 2) == 0
+        slot = jnp.where(even, k, length)
         pair_copy(s).wait_recv()
         rows = rows_ref[s, :, :width]
         grads = rows_ref[s, :, width : 2 * width]
@@ -339,44 +374,62 @@
         share_out[s, :, :width] = back[count:].astype(jnp.bfloat16)
         share_out[s, :, width:] = sums[count:].astype(jnp.bfloat16)
         share_copy(s).start()
-        keep[lax.rem(s, 2), :, :width] = back[:count]
-        keep[lax.rem(s, 2), :, width:] = sums[:count]
-
-        @pl.when(s == 1)
-        def _():
-            keep[2] = finish(0)
-
-        @pl.when(s > 1)
-        def _():
-            send_back(s - 1)
+
+        @pl.when(s > 0)
+        def _():
+            finish(s - 1)
+
+        keep[slot, :, :width] = back[:count]
+        keep[slot, :, width:] = sums[:count]
+
+        @pl.when(even & (k < length - 1))
+        def _():
+            line_copy(k + 1).wait_recv()
+            side_copy(k + 1).start()
+            pair_copy(s + 2).start()
+
+        @pl.when(even)
+        def _():
+            side_copy(k).wait_recv()
+            pair_copy(s + 1).start()
 
         acc_gate[...] += contract(grad_gate, rows, 0, 0)
         acc_up[...] += contract(grad_up, rows, 0, 0)
         acc_down[...] += contract(weighted, grads, 0, 0)
+
+        @pl.when((s > 2) & (lax.rem(s, 2) == 1))
+        def _():
+            send_back(k - 1)
+
         return carry
 
     lax.fori_loop(0, node_count, advance, 0)
-    send_back(node_count - 1)
+    finish(node_count - 1)
     dgate_ref[...] = acc_gate[...].astype(jnp.bfloat16)
     dup_ref[...] = acc_up[...].astype(jnp.bfloat16)
     ddown_ref[...] = acc_down[...].astype(jnp.bfloat16)
-    for s in range(1, node_count):
-        back_copy(s).wait_recv()
-        keep[2] += back_in[s].astype(jnp.float32)
-    tokens_ref[...] = keep[2, :, :width].astype(jnp.bfloat16)
-    table_ref[...] = keep[2, :, width:]
+    send_back(length - 1)
+    for k in range(1, length):
+        line_back(k).wait_recv()
+        keep[0] += line_in[k].astype(jnp.float32)
+    tokens_ref[...] = keep[0, :, :width].astype(jnp.bfloat16)
+    table_ref[...] = keep[0, :, width:]
     for s in range(node_count):
         pair_copy(s).wait_send()
         share_copy(s).wait_send()
-        if s > 0:
-            row_copy(s).wait_send()
-            back_copy(s).wait_send()
+    for k in range(length):
+        side_copy(k).wait_send()
+        side_back(k).wait_send()
+        if k > 0:
+            line_copy(k).wait_send()
+            line_back(k).wait_send()
 
 
 def fused(node_count, payload, gate, up, down, pick):
     count = payload.shape[0]
     units, width = down.shape
     wide = width + LANES
+    length = node_count // 2
     vmem = pl.BlockSpec(memory_space=pltpu.VMEM)
     total = 2 * count * node_count
     return pl.pallas_call(
@@ -395,10 +448,13 @@
             pltpu.VMEM(down.shape, jnp.float32),
             pltpu.VMEM(down.shape, jnp.float32),
             pltpu.VMEM(down.shape, jnp.float32),
-            pltpu.VMEM((3, count, wide), jnp.float32),
+            pltpu.VMEM((length + 1, count, wide), jnp.float32),
         ]
-        + [pltpu.VMEM((node_count, count, wide), jnp.bfloat16)] * 4
-        + [pltpu.SemaphoreType.DMA((node_count,))] * 8,
+        + [pltpu.VMEM((node_count, count, wide), jnp.bfloat16)] * 2
+        + [pltpu.VMEM((length, count, wide), jnp.bfloat16)] * 4
+        + [pltpu.SemaphoreType.DMA((length,))] * 4
+        + [pltpu.SemaphoreType.DMA((node_count,))] * 4
+        + [pltpu.SemaphoreType.DMA((length,))] * 4,
         compiler_params=pltpu.CompilerParams(
             collective_id=0, has_side_effects=True, vmem_limit_bytes=60 * 1024 * 1024
         ),
@@ -413,7 +469,7 @@
 def on_device(tokens, grad_out, expert_ids, gate_values, w_gate, w_up, w_down):
     node_count = lax.axis_size("node")
     group_size, width, half = w_gate.shape
-    if node_count > 2 * LIMIT or group_size * node_count > LANES:
+    if node_count > 2 * LIMIT or node_count % 2 or group_size * node_count > LANES:
         return routed_on_device(tokens, grad_out, expert_ids, gate_values, w_gate, w_up, w_down)
     token_count = tokens.shape[0]
     units = group_size * half

time: 191 us -> 135 us (0.71)
  Pallas kernels: 176 us -> 120 us
    pallas_call x1, Pallas kernels: 176 us -> 120 us  [fused(): pl.pallas_call(functools.partial(fused_kernel, node_count), in_specs=[vme...]
where the time goes in v3:
time: 135 us
  Pallas kernels  120 us (89%)
  local copies, waits for them, and re-layouts  9.81 us (7%)
  other arithmetic  4.17 us (3%)
    pallas_call x1, Pallas kernels, fused(): pl.pallas_call(functools.partial(fused_kernel, node_count), in_specs=[vme...  120 us
    unnamed x10, local copies, waits for them, and re-layouts  9.03 us

profile of v3, /device:TPU:0, one launch (start us, length us, event | category | flops | bytes accessed | tf_op | source)
XLA Modules:
  0.0 134.7 jit_solution(13398363146100650784)
XLA Ops:
  0.7 0.8 copy.14
  1.4 0.8 copy.15
  2.2 0.4 select_reduce_fusion.1
  2.6 0.7 fusion.pick_ref
  3.3 1.9 %pad_maximum_fusion.payload_ref = bf16[128,2176]{1,0:T(8,128)(2,1)} fusion(bf16[128,128]{1,0:T(8,128)(2,1)S(1)} %select_reduce_fusion.1, bf16[128,1024]{1,0:T(8,128)(2,1)} %param.8, bf16[128,1024]{1,0:T(8,128)(2,1)} %param.7), kind=kLoop, calls=%fused_computation | loop fusion | flops 1671168 | bytes 1114112 | tf_op jit(solution)/shard_map/concatenate | solution.py:479
  5.2 120.1 %shard_map.110 = (bf16[128,1024]{1,0:T(8,128)(2,1)}, f32[128,128]{1,0:T(8,128)}, bf16[768,1024]{1,0:T(8,128)(2,1)}, bf16[768,1024]{1,0:T(8,128)(2,1)}, bf16[768,1024]{1,0:T(8,128)(2,1)}) custom-call(bf16[128,2176]{1,0:T(8,128)(2,1)} %pad_maximum_fusion.payload_ref, bf16[768,1024]{1,0:T(8,128)(2,1)} %bitcast.17, bf16[768,1024]{1,0:T(8,128)(2,1)} %bitcast.18, ...), custom_call_target="tpu_custom_call" | custom-call | flops 25769803776 | bytes 9437184 | tf_op jit(solution)/shard_map/pallas_call | solution.py:435
  125.3 1.2 select_reduce_fusion
  126.5 0.7 copy.16
  127.1 1.7 %copy.21 = bf16[128,1024]{1,0:T(8,128)(2,1)} copy(bf16[128,1024]{1,0:T(8,128)(2,1)} %get-tuple-element.25) | data formatting | bytes 524288
  128.8 0.0 copy-start.1
  128.8 2.8 %copy.22 = bf16[4,1024,192]{1,2,0:T(8,128)(2,1)} copy(bf16[4,1024,192]{1,2,0:T(8,128)(2,1)} %bitcast.16) | data formatting | bytes 3145728
  131.6 0.0 copy-done.1
  131.6 0.0 copy-start
  131.6 1.1 copy.23
  132.8 0.8 copy-done
  133.6 1.1 copy.24
  (1 shorter events, 0.0 us)
Async XLA Ops:
  128.8 2.8 %copy-start.1 = (bf16[768,1024]{1,0:T(8,128)(2,1)S(1)}, bf16[768,1024]{1,0:T(8,128)(2,1)}, u32[]{:S(2)}) copy-start(bf16[768,1024]{1,0:T(8,128)(2,1)} %get-tuple-element.13) | copy-start | bytes 4718596
  131.6 2.0 %copy-start = (bf16[768,1024]{1,0:T(8,128)(2,1)S(1)}, bf16[768,1024]{1,0:T(8,128)(2,1)}, u32[]{:S(2)}) copy-start(bf16[768,1024]{1,0:T(8,128)(2,1)} %get-tuple-element.14) | copy-start | bytes 4718596
